TPU v7x, 512 devices: a whole 4x4x16 slice. The times are simulated.
512 devices in a mesh: dp: 32 (over x, y, core), expert: 16 (over z).
Axes of the slice: x: 4, y: 4, z: 16, core: 2. Of those that a mesh axis runs over, the one named last changes fastest.
Arguments:
- grad_out: bfloat16 [2048, 6144], P('expert', 'dp'), may hold values from -48 to 48
- routes: int32 [2048, 4], P('expert'), may hold values from 0 to 15, all different within a row; in each aligned block of 128 rows (0 to 127, 128 to 255, ...) at most 40 rows name the same one
- probs: float32 [2048, 4], P('expert'), may hold values from 0.05 to 0.6
- resp_len: int32 [16, 4], P('expert'), may hold values from 1 to 64, 128 in all within a row
- w_down: bfloat16 [16, 5376, 6144], P('expert', 'dp'), may hold values from -0.078125 to 0.078125
- w_up: bfloat16 [16, 6144, 5376], P('expert', 'dp'), may hold values from -0.078125 to 0.078125
- gate_act: bfloat16 [16, 640, 5376], P('expert', None, 'dp'), may hold values from -6 to 6
Outputs:
- grad_in: bfloat16 [2048, 6144], P('expert', 'dp')
Inputs may be any that keep to these rules, and one draw needn't show every extreme that they name: `routes`: within each aligned block of 128 rows (one shard) no expert is named more than 40 times, a bound that some block reaches. `resp_len`: each row sums to 128, and its largest entry is 64.
All inputs are finite; a program needn't handle non-finite values.
Results may differ from a plain program's by a relative error of at most 0.013.
Values may be sent and summed in bfloat16 or wider, within the bound.
No kernel may reach another device: no remote copies, remote signals or barrier semaphores. Data moves between devices by JAX's collectives and lax.ppermute only.
A program may use at most 64 MiB of HBM per device.

v0:
```python
import jax
import jax.numpy as jnp
from jax import lax
from jax.sharding import PartitionSpec as P


def token_weight(resp_len, rows):
    lengths = resp_len[0]
    ends = jnp.cumsum(lengths)
    starts = ends - lengths
    position = jnp.arange(rows, dtype=jnp.int32)[:, None]
    inside = (position >= starts[None, :]) & (position < ends[None, :])
    inverse = 1.0 / lengths.astype(jnp.float32)
    return jnp.sum(jnp.where(inside, inverse[None, :], jnp.zeros_like(inverse)[None, :]), axis=1)


def slot_index(routes, experts, capacity):
    labels = jnp.arange(experts, dtype=jnp.int32)
    hits = (routes[:, :, None] == labels[None, None, :]).astype(jnp.int32)
    per_row = jnp.sum(hits, axis=1)
    before = jnp.cumsum(per_row, axis=0) - per_row
    position = jnp.sum(hits * before[:, None, :], axis=2)
    return routes * capacity + position


def contract(left, right):
    return lax.dot_general(
        left, right, (((1,), (1,)), ((), ())), preferred_element_type=jnp.float32
    )


def on_device(grad_out, routes, probs, resp_len, w_down, w_up, gate_act):
    tokens_here, width_here = grad_out.shape
    picks = routes.shape[1]
    experts = lax.axis_size("expert")
    capacity = min(
        tokens_here, tokens_here * picks // experts + tokens_here * picks // (4 * experts)
    )
    slots = experts * capacity
    weight = token_weight(resp_len, tokens_here)
    target = slot_index(routes, experts, capacity).reshape(-1)
    factor = probs * weight[:, None]
    scaled = (grad_out[:, None, :].astype(jnp.float32) * factor[:, :, None]).astype(jnp.bfloat16)
    selector = (jnp.arange(slots, dtype=jnp.int32)[:, None] == target[None, :]).astype(jnp.bfloat16)
    outgoing = jnp.dot(
        selector,
        scaled.reshape(tokens_here * picks, width_here),
        preferred_element_type=jnp.float32,
    ).astype(jnp.bfloat16)
    arrived = lax.all_to_all(
        outgoing.reshape(experts, capacity, width_here),
        "expert",
        split_axis=0,
        concat_axis=0,
        tiled=True,
    ).reshape(slots, width_here)
    down_rows = w_down[0]
    up_rows = w_up[0]
    saved = gate_act[0]
    full_rows = lax.all_gather(arrived, "dp", axis=1, tiled=True)
    hidden_sum = contract(full_rows, down_rows)
    hidden_grad = (hidden_sum * saved.astype(jnp.float32)).astype(jnp.bfloat16)
    full_hidden = lax.all_gather(hidden_grad, "dp", axis=1, tiled=True)
    product = contract(full_hidden, up_rows)
    returning = product.astype(jnp.bfloat16)
    back = lax.all_to_all(
        returning.reshape(experts, capacity, width_here),
        "expert",
        split_axis=0,
        concat_axis=0,
        tiled=True,
    ).reshape(slots, width_here)
    picked = (
        jnp.take(back, target, axis=0).reshape(tokens_here, picks, width_here).astype(jnp.float32)
    )
    return jnp.sum(picked, axis=1).astype(jnp.bfloat16)


def solution(mesh):
    in_specs = (
        P("expert", "dp"),
        P("expert", None),
        P("expert", None),
        P("expert", None),
        P("expert", "dp", None),
        P("expert", "dp", None),
        P("expert", None, "dp"),
    )
    out_specs = P("expert", "dp")
    return jax.shard_map(
        on_device, mesh=mesh, in_specs=in_specs, out_specs=out_specs, check_vma=False
    )
```

profile of v0, /device:TPU:2, one launch (start us, length us, event | category | flops | bytes accessed | tf_op | source)
XLA Modules:
  0.0 234.0 jit_solution(2945897742113075317)
XLA Ops:
  6.5 0.8 divide_bitcast_fusion
  7.3 0.8 reduce-window.4
  8.2 0.7 fusion.18
  8.8 0.7 convert_reduce_fusion
  9.7 0.7 broadcast_multiply_fusion
  10.6 0.2 reduce_window_sum.18
  10.9 0.7 select_reduce_fusion.1
  11.6 0.7 compare_and_fusion
  12.5 0.9 copy.35
  13.5 0.2 mul.48
  13.7 0.5 fusion.8
  14.2 0.2 copy.37
  14.4 35.8 %all_to_all.10 = bf16[16,40,192]{2,1,0:T(8,128)(2,1)S(1)} all-to-all(bf16[16,40,192]{2,1,0:T(8,128)(2,1)S(1)} %bitcast.33), channel_id=1, replica_groups=mesh['dp'=32,'expert'=16] {'expert'}, dimensions={0} | all-to-all | bytes 491520 | tf_op jit(solution)/shard_map/all_to_all | solution.py:50
  50.2 0.9 copy.38
  51.1 62.5 %all-gather.3.cloned.1.call-done = bf16[640,6144]{0,1:T(8,128)(2,1)} async-done(((bf16[640,192]{0,1:T(8,128)(2,1)}), bf16[640,6144]{0,1:T(8,128)(2,1)}) %all-gather.3.cloned.1.call-update) | async-done | bytes 7864336 | tf_op jit(solution)/shard_map/all_gather | solution.py:60
  113.6 6.3 %fusion.12 = bf16[640,168]{0,1:T(8,128)(2,1)} fusion(bf16[640,6144]{0,1:T(8,128)(2,1)} %all-gather.3.cloned.1.call-done, bf16[1,168,6144]{2,1,0:T(8,128)(2,1)} %param.11, bf16[1,640,168]{1,2,0:T(8,128)(2,1)} %param.13), kind=kOutput, calls=%fused_computation.10 | convolution fusion | flops 1321528320 | bytes 10358784 | tf_op jit(solution)/shard_map/dot_general | solution.py:27
  120.0 64.6 %all-gather.5.cloned.1.call-done = bf16[640,5376]{0,1:T(8,128)(2,1)} async-done(((bf16[640,168]{0,1:T(8,128)(2,1)}), bf16[640,5376]{0,1:T(8,128)(2,1)}) %all-gather.5.cloned.1.call-update) | async-done | bytes 6881296 | tf_op jit(solution)/shard_map/all_gather | solution.py:63
  184.6 4.7 %fusion.9 = bf16[640,192]{0,1:T(8,128)(2,1)S(1)} fusion(bf16[640,5376]{0,1:T(8,128)(2,1)} %all-gather.5.cloned.1.call-done, bf16[1,192,5376]{2,1,0:T(8,128)(2,1)S(1)} %copy-done), kind=kOutput, calls=%fused_computation.9 | convolution fusion | flops 1321328640 | bytes 9191424 | tf_op jit(solution)/shard_map/dot_general | solution.py:27
  189.3 0.9 copy.39
  190.2 12.3 %all-to-all-start.1 = ((bf16[16,40,192]{2,1,0:T(8,128)(2,1)}), bf16[16,40,192]{2,1,0:T(8,128)(2,1)S(1)}, u32[]{:S(2)}, u32[]{:S(2)}) async-start(bf16[16,40,192]{2,1,0:T(8,128)(2,1)} %bitcast.10), calls=%async_computation.1 | async-start | bytes 655360 | tf_op jit(solution)/shard_map/all_to_all | solution.py:66
  202.8 21.2 %all-to-all-done.1 = bf16[16,40,192]{2,1,0:T(8,128)(2,1)S(1)} async-done(((bf16[16,40,192]{2,1,0:T(8,128)(2,1)}), bf16[16,40,192]{2,1,0:T(8,128)(2,1)S(1)}, u32[]{:S(2)}, u32[]{:S(2)}) %all-to-all-start.1) | async-done | bytes 245792 | tf_op jit(solution)/shard_map/all_to_all | solution.py:66
  224.0 1.9 gather_fusion
  226.1 0.4 select_reduce_fusion
  226.4 0.7 copy.41
  (20 shorter events, 1.2 us)
Async XLA Ops:
  6.5 178.1 %copy-start = (bf16[1,192,5376]{2,1,0:T(8,128)(2,1)S(1)}, bf16[1,192,5376]{2,1,0:T(8,128)(2,1)}, u32[]{:S(2)}) copy-start(bf16[1,192,5376]{2,1,0:T(8,128)(2,1)} %param.12) | copy-start | bytes 6193156
  6.5 107.1 %all-gather.3.cloned.1.call-start = ((), (), s32[]{:S(2)}) async-start(), calls=%async_computation.2 | async-start | bytes 8110080 | tf_op jit(solution)/shard_map/all_gather | solution.py:60
  51.0 133.6 %all-gather.5.cloned.1.call-start = ((), (), s32[]{:S(2)}) async-start(), calls=%async_computation.3 | async-start | bytes 7096320 | tf_op jit(solution)/shard_map/all_gather | solution.py:63
  190.2 33.8 %all-to-all-start.1 = ((bf16[16,40,192]{2,1,0:T(8,128)(2,1)}), bf16[16,40,192]{2,1,0:T(8,128)(2,1)S(1)}, u32[]{:S(2)}, u32[]{:S(2)}) async-start(bf16[16,40,192]{2,1,0:T(8,128)(2,1)} %bitcast.10), calls=%async_computation.1 | async-start | bytes 655360 | tf_op jit(solution)/shard_map/all_to_all | solution.py:66
Sparse Core Ops, SparseCore 0:
  51.2 62.4 all-gather.2
  120.1 64.4 all-gather.4
where the time goes:
time: 234 us
  waiting for transfers between devices  148 us (63%)
  blocking collectives  35.8 us (15%)
  between operations  13.5 us (6%)
  starting transfers between devices  12.3 us (5%)
  matrix products  11.5 us (5%)
  local copies, waits for them, and re-layouts  6.7 us (3%)
  other arithmetic  5.74 us (2%)
    all_gather x1, waiting for transfers between devices, on_device(): full_hidden = lax.all_gather(hidden_grad, 'dp', axis=1, tiled=True)  64.6 us
    all_gather x1, waiting for transfers between devices, on_device(): full_rows = lax.all_gather(arrived, 'dp', axis=1, tiled=True)  62.5 us
    all_to_all x1, blocking collectives, on_device(): lax.all_to_all(outgoing.reshape(experts, capacity, width_here), 'expert',...  35.8 us
    all_to_all x1, waiting for transfers between devices, on_device(): lax.all_to_all(returning.reshape(experts, capacity, width_here), 'expert'...  21.2 us
    all_to_all x1, starting transfers between devices, on_device(): lax.all_to_all(returning.reshape(experts, capacity, width_here), 'expert'...  12.3 us
    dot_general x2, matrix products, contract(): lax.dot_general(left, right, (((1,), (1,)), ((), ())), preferred_element_...  11 us
  transfers between devices with their start and end apart: 3, of which 3 were waited for; matrix products, arithmetic and copies ran while one was open for 0% of the time, Pallas kernels for 0%

commit v1 on v0

--- a/solution.py
+++ b/solution.py
@@ -57,7 +57,9 @@
     down_rows = w_down[0]
     up_rows = w_up[0]
     saved = gate_act[0]
-    full_rows = lax.all_gather(arrived, "dp", axis=1, tiled=True)
+    full_rows = jnp.concatenate(
+        lax.all_to_all(jnp.stack([arrived] * lax.axis_size("dp")), "dp", 0, 0), axis=1
+    )
     hidden_sum = contract(full_rows, down_rows)
     hidden_grad = (hidden_sum * saved.astype(jnp.float32)).astype(jnp.bfloat16)
     full_hidden = lax.all_gather(hidden_grad, "dp", axis=1, tiled=True)

time: 234 us -> 258 us (1.10)
  blocking collectives: 35.8 us -> 132 us
  waiting for transfers between devices: 148 us -> 79.5 us
  matrix products: 11.5 us -> 7.83 us
    all_to_all x0 -> x1, blocking collectives: none -> 95.9 us  [on_device(): lax.all_to_all(jnp.stack([arrived] * lax.axis_size('dp')), 'dp', 0, 0)]
    all_gather x1 -> x0, waiting for transfers between devices: 62.5 us -> none  [on_device(): full_rows = lax.all_gather(arrived, 'dp', axis=1, tiled=True)]
    all_gather x1, waiting for transfers between devices: 64.6 us -> 58.3 us  [on_device(): full_hidden = lax.all_gather(hidden_grad, 'dp', axis=1, tiled=True)]
    dot_general x2, matrix products: 11 us -> 7.33 us  [contract(): lax.dot_general(left, right, (((1,), (1,)), ((), ())), preferred_element_...]
  transfers between devices with their start and end apart: 3 -> 2, of which waited for: 3 -> 2; matrix products, arithmetic and copies ran while one was open for 0% -> 0% of each run, Pallas kernels for 0% -> 0%
where the time goes in v1:
time: 258 us
  blocking collectives  132 us (51%)
  waiting for transfers between devices  79.5 us (31%)
  between operations  13.5 us (5%)
  starting transfers between devices  12.3 us (5%)
  matrix products  7.83 us (3%)
  local copies, waits for them, and re-layouts  7.09 us (3%)
  other arithmetic  5.74 us (2%)
    all_to_all x1, blocking collectives, on_device(): lax.all_to_all(jnp.stack([arrived] * lax.axis_size('dp')), 'dp', 0, 0)  95.9 us
    all_gather x1, waiting for transfers between devices, on_device(): full_hidden = lax.all_gather(hidden_grad, 'dp', axis=1, tiled=True)  58.3 us
    all_to_all x1, blocking collectives, on_device(): lax.all_to_all(outgoing.reshape(experts, capacity, width_here), 'expert',...  35.8 us
    all_to_all x1, waiting for transfers between devices, on_device(): lax.all_to_all(returning.reshape(experts, capacity, width_here), 'expert'...  21.2 us
    all_to_all x1, starting transfers between devices, on_device(): lax.all_to_all(returning.reshape(experts, capacity, width_here), 'expert'...  12.3 us
    dot_general x2, matrix products, contract(): lax.dot_general(left, right, (((1,), (1,)), ((), ())), preferred_element_...  7.33 us
  transfers between devices with their start and end apart: 2, of which 2 were waited for; matrix products, arithmetic and copies ran while one was open for 0% of the time, Pallas kernels for 0%

profile of v1, /device:TPU:2, one launch (start us, length us, event | category | flops | bytes accessed | tf_op | source)
XLA Modules:
  0.0 257.6 jit_solution(14835909791957190649)
XLA Ops:
  6.5 0.8 divide_bitcast_fusion
  7.3 0.8 reduce-window.4
  8.2 0.7 fusion.18
  8.8 0.7 convert_reduce_fusion
  9.7 0.7 broadcast_multiply_fusion
  10.9 0.7 select_reduce_fusion.1
  11.6 0.7 compare_and_fusion
  12.5 0.9 copy.37
  13.5 0.2 mul.48
  13.7 0.5 fusion.8
  14.2 0.2 copy.39
  14.4 35.8 %all_to_all.15 = bf16[16,40,192]{2,1,0:T(8,128)(2,1)S(1)} all-to-all(bf16[16,40,192]{2,1,0:T(8,128)(2,1)S(1)} %bitcast.37), channel_id=1, replica_groups=mesh['dp'=32,'expert'=16] {'expert'}, dimensions={0} | all-to-all | bytes 491520 | tf_op jit(solution)/shard_map/all_to_all | solution.py:50
  50.2 0.2 copy.40
  50.3 1.1 stack.3
  51.4 95.9 %all_to_all.16 = bf16[32,640,192]{1,2,0:T(8,128)(2,1)S(1)} all-to-all(bf16[32,640,192]{1,2,0:T(8,128)(2,1)S(1)} %stack.3), channel_id=1, replica_groups=mesh['dp'=32,'expert'=16] {'dp'}, dimensions={0} | all-to-all | bytes 15728640 | tf_op jit(solution)/shard_map/all_to_all | solution.py:61
  147.3 2.6 %fusion.12 = bf16[640,168]{0,1:T(8,128)(2,1)} fusion(bf16[640,6144]{0,1:T(8,128)(2,1)S(1)} %bitcast.36, bf16[1,168,6144]{2,1,0:T(8,128)(2,1)S(1)} %copy-done.1, bf16[1,640,168]{1,2,0:T(8,128)(2,1)S(1)} %copy-done.2), kind=kOutput, calls=%fused_computation.10 | convolution fusion | flops 1321528320 | bytes 10358784 | tf_op jit(solution)/shard_map/dot_general | solution.py:27
  149.9 58.3 %all-gather.2.cloned.1.call-done = bf16[640,5376]{0,1:T(8,128)(2,1)} async-done(((bf16[640,168]{0,1:T(8,128)(2,1)}), bf16[640,5376]{0,1:T(8,128)(2,1)}) %all-gather.2.cloned.1.call-update) | async-done | bytes 6881296 | tf_op jit(solution)/shard_map/all_gather | solution.py:65
  208.2 4.7 %fusion.9 = bf16[640,192]{0,1:T(8,128)(2,1)S(1)} fusion(bf16[640,5376]{0,1:T(8,128)(2,1)} %all-gather.2.cloned.1.call-done, bf16[1,192,5376]{2,1,0:T(8,128)(2,1)S(1)} %copy-done), kind=kOutput, calls=%fused_computation.9 | convolution fusion | flops 1321328640 | bytes 9191424 | tf_op jit(solution)/shard_map/dot_general | solution.py:27
  213.0 0.9 copy.41
  213.9 12.3 %all-to-all-start.2 = ((bf16[16,40,192]{2,1,0:T(8,128)(2,1)}), bf16[16,40,192]{2,1,0:T(8,128)(2,1)S(1)}, u32[]{:S(2)}, u32[]{:S(2)}) async-start(bf16[16,40,192]{2,1,0:T(8,128)(2,1)} %bitcast.12), calls=%async_computation.2 | async-start | bytes 655360 | tf_op jit(solution)/shard_map/all_to_all | solution.py:68
  226.4 21.2 %all-to-all-done.2 = bf16[16,40,192]{2,1,0:T(8,128)(2,1)S(1)} async-done(((bf16[16,40,192]{2,1,0:T(8,128)(2,1)}), bf16[16,40,192]{2,1,0:T(8,128)(2,1)S(1)}, u32[]{:S(2)}, u32[]{:S(2)}) %all-to-all-start.2) | async-done | bytes 245792 | tf_op jit(solution)/shard_map/all_to_all | solution.py:68
  247.6 1.9 gather_fusion
  249.7 0.4 select_reduce_fusion
  250.1 0.7 copy.43
  (23 shorter events, 1.3 us)
Async XLA Ops:
  6.5 201.7 %copy-start = (bf16[1,192,5376]{2,1,0:T(8,128)(2,1)S(1)}, bf16[1,192,5376]{2,1,0:T(8,128)(2,1)}, u32[]{:S(2)}) copy-start(bf16[1,192,5376]{2,1,0:T(8,128)(2,1)} %param.12) | copy-start | bytes 6193156
  6.5 201.7 %all-gather.2.cloned.1.call-start = ((), (), s32[]{:S(2)}) async-start(), calls=%async_computation.3 | async-start | bytes 7096320 | tf_op jit(solution)/shard_map/all_gather | solution.py:65
  51.4 95.9 %copy-start.1 = (bf16[1,168,6144]{2,1,0:T(8,128)(2,1)S(1)}, bf16[1,168,6144]{2,1,0:T(8,128)(2,1)}, u32[]{:S(2)}) copy-start(bf16[1,168,6144]{2,1,0:T(8,128)(2,1)} %param.11) | copy-start | bytes 6193156
  51.4 95.9 %copy-start.2 = (bf16[1,640,168]{1,2,0:T(8,128)(2,1)S(1)}, bf16[1,640,168]{1,2,0:T(8,128)(2,1)}, u32[]{:S(2)}) copy-start(bf16[1,640,168]{1,2,0:T(8,128)(2,1)} %param.13) | copy-start | bytes 645124
  213.9 33.8 %all-to-all-start.2 = ((bf16[16,40,192]{2,1,0:T(8,128)(2,1)}), bf16[16,40,192]{2,1,0:T(8,128)(2,1)S(1)}, u32[]{:S(2)}, u32[]{:S(2)}) async-start(bf16[16,40,192]{2,1,0:T(8,128)(2,1)} %bitcast.12), calls=%async_computation.2 | async-start | bytes 655360 | tf_op jit(solution)/shard_map/all_to_all | solution.py:68
Sparse Core Ops, SparseCore 0:
  150.1 58.1 all-gather.1
